TPU v7x, 128 devices: a whole 4x4x4 slice. The times are simulated.
128 devices in a mesh: dp: 64 (over z_hi, x, y, core), tensor: 2 (over z_lo).
Axes of the slice: x: 4, y: 4, z: 4 (z_hi: 2, z_lo: 2; z = z_hi * 2 + z_lo), core: 2. Of those that a mesh axis runs over, the one named last changes fastest.
Arguments:
- layer_input: bfloat16 [32768, 768], P('dp'), may hold values from -6 to 6
- seg_ids: int32 [32768], P('dp'), may hold values from 0 to 127, never falling along the last dimension, each value on 1 to 2048 neighbouring positions
- ln1_gain: float32 [768], replicated, may hold values from 0.5 to 1.5
- ln1_bias: float32 [768], replicated, may hold values from -2.5 to 2.5
- ln2_gain: float32 [768], replicated, may hold values from 0.5 to 1.5
- ln2_bias: float32 [768], replicated, may hold values from -2.5 to 2.5
- w_qkv: bfloat16 [768, 12, 192], P(None, 'tensor'), may hold values from -0.21875 to 0.21875
- b_qkv: float32 [12, 192], P('tensor'), may hold values from -2.5 to 2.5
- w_out: bfloat16 [12, 64, 768], P('tensor'), may hold values from -0.625 to 0.625
- b_out: float32 [768], replicated, may hold values from -2.5 to 2.5
- w_fc: bfloat16 [768, 3072], P(None, 'tensor'), may hold values from -0.21875 to 0.21875
- b_fc: float32 [3072], P('tensor'), may hold values from -2.5 to 2.5
- w_proj: bfloat16 [3072, 768], P('tensor'), may hold values from -0.109375 to 0.109375
- b_proj: float32 [768], replicated, may hold values from -2.5 to 2.5
- cotangent: float32 [32768, 768], P('dp'), may hold values from -6 to 6
Outputs:
- layer_output: bfloat16 [32768, 768], P('dp')
- grad_input: float32 [32768, 768], P('dp')
- grad_ln1_gain: float32 [768], replicated
- grad_ln1_bias: float32 [768], replicated
- grad_ln2_gain: float32 [768], replicated
- grad_ln2_bias: float32 [768], replicated
- grad_w_qkv: float32 [768, 12, 192], P(None, 'tensor')
- grad_b_qkv: float32 [12, 192], P('tensor')
- grad_w_out: float32 [12, 64, 768], P('tensor')
- grad_b_out: float32 [768], replicated
- grad_w_fc: float32 [768, 3072], P(None, 'tensor')
- grad_b_fc: float32 [3072], P('tensor')
- grad_w_proj: float32 [3072, 768], P('tensor')
- grad_b_proj: float32 [768], replicated
Inputs may be any that keep to these rules, and one draw needn't show every extreme that they name: `seg_ids`: document numbers never fall from one token to the next.
All inputs are finite; a program needn't handle non-finite values.
Results may differ from a plain program's by a relative error of at most 0.0098.
Values may be sent and summed in bfloat16 or wider, within the bound.
No kernel may reach another device: no remote copies, remote signals or barrier semaphores. Data moves between devices by JAX's collectives and lax.ppermute only.
A program may use at most 128 MiB of HBM per device.

v0:
```python
import jax
import jax.numpy as jnp
from jax import lax
from jax.sharding import PartitionSpec as P

HD = 64
ROT = 16
SEQ = 512
epsilon = 1e-05
masked_score = -1000000000.0


def norm_rows(row_values, gain_vec, shift_vec):
    row_mean = jnp.mean(row_values, axis=-1, keepdims=True)
    centred = row_values - row_mean
    variance = jnp.mean(centred * centred, axis=-1, keepdims=True)
    return centred * lax.rsqrt(variance + epsilon) * gain_vec + shift_vec


def rotate(row_values, cosine_table, sine_table):
    half_rot = ROT // 2
    leading = row_values[..., :half_rot]
    trailing = row_values[..., half_rot:ROT]
    cosine_col = cosine_table[:, None, :]
    sine_col = sine_table[:, None, :]
    return jnp.concatenate(
        [
            leading * cosine_col - trailing * sine_col,
            trailing * cosine_col + leading * sine_col,
            row_values[..., ROT:],
        ],
        axis=-1,
    )


def tables(segments):
    indices = jnp.arange(SEQ, dtype=jnp.int32)
    starts = jnp.concatenate([jnp.ones((1,), dtype=bool), segments[1:] != segments[:-1]])
    opening = lax.cummax(jnp.where(starts, indices, 0), axis=0)
    offset = (indices - opening).astype(jnp.float32)
    frequency = 10000.0 ** (jnp.arange(ROT // 2).astype(jnp.float32) * (-2.0 / ROT))
    angles = offset[:, None] * frequency[None, :]
    allowed = (segments[:, None] == segments[None, :]) & (indices[:, None] >= indices[None, :])
    return (jnp.cos(angles), jnp.sin(angles), allowed)


def gelu_exact(row_values):
    return jax.nn.gelu(row_values, approximate=False)


def contract_rows(left_mat, right_mat):
    return lax.dot_general(
        left_mat, right_mat, (((0,), (0,)), ((), ())), preferred_element_type=jnp.float32
    )


def contract_cols(left_mat, right_mat):
    return lax.dot_general(
        left_mat, right_mat, (((1,), (1,)), ((), ())), preferred_element_type=jnp.float32
    )


def body(
    layer_input,
    seg_ids,
    ln1_gain,
    ln1_bias,
    ln2_gain,
    ln2_bias,
    w_qkv,
    b_qkv,
    w_out,
    b_out,
    w_fc,
    b_fc,
    w_proj,
    b_proj,
    cotangent,
):
    tok_rows = layer_input.shape[0]
    model_width = layer_input.shape[1]
    head_count = w_qkv.shape[1]
    seq_count = tok_rows // SEQ
    score_scale = HD ** (-0.5)
    x_float = layer_input.astype(jnp.float32)
    normed_attn, pull_attn = jax.vjp(norm_rows, x_float, ln1_gain, ln1_bias)
    normed_mlp, pull_mlp = jax.vjp(norm_rows, x_float, ln2_gain, ln2_bias)
    attn_in = normed_attn.astype(jnp.bfloat16)
    mlp_in = normed_mlp.astype(jnp.bfloat16)
    flat_qkv = w_qkv.reshape(model_width, head_count * 3 * HD)
    mixed_qkv = (
        jnp.dot(attn_in, flat_qkv, preferred_element_type=jnp.float32).reshape(
            tok_rows, head_count, 3 * HD
        )
        + b_qkv
    )
    hidden = jnp.dot(mlp_in, w_fc, preferred_element_type=jnp.float32) + b_fc
    activated, pull_gelu = jax.vjp(gelu_exact, hidden)
    act_low = activated.astype(jnp.bfloat16)
    seg_blocks = seg_ids.reshape(seq_count, SEQ)

    def attend_forward(packed):
        mixed_seq, segments = packed
        cosine_table, sine_table, allowed = tables(segments)
        queries = rotate(mixed_seq[..., :HD], cosine_table, sine_table).astype(jnp.bfloat16)
        keys_rot = rotate(mixed_seq[..., HD : 2 * HD], cosine_table, sine_table).astype(
            jnp.bfloat16
        )
        values = mixed_seq[..., 2 * HD :].astype(jnp.bfloat16)
        scores = (
            jnp.einsum("qhd,khd->hqk", queries, keys_rot, preferred_element_type=jnp.float32)
            * score_scale
        )
        scores = jnp.where(allowed[None], scores, masked_score)
        row_top = jnp.max(scores, axis=-1, keepdims=True)
        powers = jnp.exp(scores - row_top)
        totals = jnp.sum(powers, axis=-1, keepdims=True)
        weights = (powers / totals).astype(jnp.bfloat16)
        context = jnp.einsum("hqk,khd->qhd", weights, values, preferred_element_type=jnp.float32)
        return (context.astype(jnp.bfloat16), row_top + jnp.log(totals), queries, keys_rot, values)

    context, log_totals, queries_all, keys_all, values_all = lax.map(
        attend_forward, (mixed_qkv.reshape(seq_count, SEQ, head_count, 3 * HD), seg_blocks)
    )
    context_flat = context.reshape(tok_rows, head_count * HD)
    flat_out = w_out.reshape(head_count * HD, model_width)
    partial_value = jnp.dot(context_flat, flat_out, preferred_element_type=jnp.float32) + jnp.dot(
        act_low, w_proj, preferred_element_type=jnp.float32
    )
    output = (
        x_float
        + lax.psum(partial_value.astype(jnp.bfloat16), "tensor").astype(jnp.float32)
        + b_out
        + b_proj
    ).astype(jnp.bfloat16)
    grad_low = cotangent.astype(jnp.bfloat16)
    grad_shift = jnp.sum(cotangent, axis=0)
    grad_w_proj = contract_rows(act_low, grad_low)
    grad_act = contract_cols(grad_low, w_proj)
    grad_hidden = pull_gelu(grad_act)[0].astype(jnp.bfloat16)
    grad_b_fc = jnp.sum(grad_hidden, axis=0, dtype=jnp.float32)
    grad_w_fc = contract_rows(mlp_in, grad_hidden)
    grad_mlp_in = contract_cols(grad_hidden, w_fc)
    grad_w_out = contract_rows(context_flat, grad_low).reshape(w_out.shape)
    grad_context = (
        contract_cols(grad_low, flat_out)
        .astype(jnp.bfloat16)
        .reshape(seq_count, SEQ, head_count, HD)
    )

    def attend_backward(packed):
        queries, keys_rot, values, log_seq, grad_seq, segments = packed
        cosine_table, sine_table, allowed = tables(segments)
        scores = (
            jnp.einsum("qhd,khd->hqk", queries, keys_rot, preferred_element_type=jnp.float32)
            * score_scale
        )
        scores = jnp.where(allowed[None], scores, masked_score)
        probabilities = jnp.exp(scores - log_seq)
        grad_values = jnp.einsum(
            "hqk,qhd->khd",
            probabilities.astype(jnp.bfloat16),
            grad_seq,
            preferred_element_type=jnp.float32,
        )
        grad_probs = jnp.einsum(
            "qhd,khd->hqk", grad_seq, values, preferred_element_type=jnp.float32
        )
        grad_scores = (
            probabilities
            * (grad_probs - jnp.sum(probabilities * grad_probs, axis=-1, keepdims=True))
        ).astype(jnp.bfloat16)
        grad_queries = (
            jnp.einsum("hqk,khd->qhd", grad_scores, keys_rot, preferred_element_type=jnp.float32)
            * score_scale
        )
        grad_keys = (
            jnp.einsum("hqk,qhd->khd", grad_scores, queries, preferred_element_type=jnp.float32)
            * score_scale
        )
        return jnp.concatenate(
            [
                rotate(grad_queries, cosine_table, -sine_table),
                rotate(grad_keys, cosine_table, -sine_table),
                grad_values,
            ],
            axis=-1,
        )

    grad_mixed = lax.map(
        attend_backward, (queries_all, keys_all, values_all, log_totals, grad_context, seg_blocks)
    )
    grad_mixed = grad_mixed.reshape(tok_rows, head_count * 3 * HD).astype(jnp.bfloat16)
    grad_b_qkv = jnp.sum(grad_mixed, axis=0, dtype=jnp.float32).reshape(head_count, 3 * HD)
    grad_w_qkv = contract_rows(attn_in, grad_mixed).reshape(w_qkv.shape)
    grad_attn_in = contract_cols(grad_mixed, flat_qkv)
    grad_x_attn, grad_gain_attn, grad_bias_attn = pull_attn(grad_attn_in)
    grad_x_mlp, grad_gain_mlp, grad_bias_mlp = pull_mlp(grad_mlp_in)
    summed_x, gain_attn, bias_attn, gain_mlp, bias_mlp = (
        lax.psum((grad_x_attn + grad_x_mlp).astype(jnp.bfloat16), "tensor").astype(jnp.float32),
        lax.psum(grad_gain_attn.astype(jnp.bfloat16), "tensor").astype(jnp.float32),
        lax.psum(grad_bias_attn.astype(jnp.bfloat16), "tensor").astype(jnp.float32),
        lax.psum(grad_gain_mlp.astype(jnp.bfloat16), "tensor").astype(jnp.float32),
        lax.psum(grad_bias_mlp.astype(jnp.bfloat16), "tensor").astype(jnp.float32),
    )
    grad_x = cotangent + summed_x
    shares = (
        lax.psum_scatter(grad_w_qkv, "dp", scatter_dimension=0, tiled=True),
        lax.psum_scatter(grad_b_qkv, "dp", scatter_dimension=1, tiled=True),
        lax.psum_scatter(grad_w_out, "dp", scatter_dimension=2, tiled=True),
        lax.psum_scatter(grad_w_fc, "dp", scatter_dimension=0, tiled=True),
        lax.psum_scatter(grad_b_fc, "dp", scatter_dimension=0, tiled=True),
        lax.psum_scatter(grad_w_proj, "dp", scatter_dimension=1, tiled=True),
        lax.psum_scatter(grad_shift, "dp", scatter_dimension=0, tiled=True),
        lax.psum_scatter(gain_attn, "dp", scatter_dimension=0, tiled=True),
        lax.psum_scatter(bias_attn, "dp", scatter_dimension=0, tiled=True),
        lax.psum_scatter(gain_mlp, "dp", scatter_dimension=0, tiled=True),
        lax.psum_scatter(bias_mlp, "dp", scatter_dimension=0, tiled=True),
    )
    whole_grads = (
        lax.all_gather(shares[0].astype(jnp.bfloat16), "dp", axis=0, tiled=True).astype(
            jnp.float32
        ),
        lax.all_gather(shares[1].astype(jnp.bfloat16), "dp", axis=1, tiled=True).astype(
            jnp.float32
        ),
        lax.all_gather(shares[2].astype(jnp.bfloat16), "dp", axis=2, tiled=True).astype(
            jnp.float32
        ),
        lax.all_gather(shares[3].astype(jnp.bfloat16), "dp", axis=0, tiled=True).astype(
            jnp.float32
        ),
        lax.all_gather(shares[4].astype(jnp.bfloat16), "dp", axis=0, tiled=True).astype(
            jnp.float32
        ),
        lax.all_gather(shares[5].astype(jnp.bfloat16), "dp", axis=1, tiled=True).astype(
            jnp.float32
        ),
        lax.all_gather(shares[6].astype(jnp.bfloat16), "dp", axis=0, tiled=True).astype(
            jnp.float32
        ),
        lax.all_gather(shares[7].astype(jnp.bfloat16), "dp", axis=0, tiled=True).astype(
            jnp.float32
        ),
        lax.all_gather(shares[8].astype(jnp.bfloat16), "dp", axis=0, tiled=True).astype(
            jnp.float32
        ),
        lax.all_gather(shares[9].astype(jnp.bfloat16), "dp", axis=0, tiled=True).astype(
            jnp.float32
        ),
        lax.all_gather(shares[10].astype(jnp.bfloat16), "dp", axis=0, tiled=True).astype(
            jnp.float32
        ),
    )
    return (
        output,
        grad_x,
        whole_grads[7],
        whole_grads[8],
        whole_grads[9],
        whole_grads[10],
        whole_grads[0],
        whole_grads[1],
        whole_grads[2],
        whole_grads[6],
        whole_grads[3],
        whole_grads[4],
        whole_grads[5],
        whole_grads[6],
    )


def solution(mesh):
    placed = (
        P("dp", None),
        P("dp"),
        P(),
        P(),
        P(),
        P(),
        P(None, "tensor", None),
        P("tensor", None),
        P("tensor", None, None),
        P(),
        P(None, "tensor"),
        P("tensor"),
        P("tensor", None),
        P(),
        P("dp", None),
    )
    return jax.shard_map(
        body,
        mesh=mesh,
        in_specs=placed,
        out_specs=(
            P("dp", None),
            P("dp", None),
            P(),
            P(),
            P(),
            P(),
            P(None, "tensor", None),
            P("tensor", None),
            P("tensor", None, None),
            P(),
            P(None, "tensor"),
            P("tensor"),
            P("tensor", None),
            P(),
        ),
        check_vma=False,
    )
```

profile of v0, /device:TPU:1, one launch (start us, length us, event | category | flops | bytes accessed | tf_op | source)
XLA Modules:
  0.0 1356.6 jit_solution(9484674918558623280)
XLA Ops:
  13.5 4.4 fusion.88
  37.0 9.2 convert_reduce_fusion
  58.5 5.3 fusion.51
  64.2 3.5 fusion.55
  69.0 5.3 all-reduce.21
  74.3 370.4 %all-reduce.28 = (bf16[768]{0:T(1024)(128)(2,1)}, bf16[768]{0:T(1024)(128)(2,1)}, bf16[768]{0:T(1024)(128)(2,1)}, bf16[768]{0:T(1024)(128)(2,1)}, bf16[768,6,192...) all-reduce(bf16[768]{0:T(1024)(128)(2,1)S(1)} %get-tuple-element.14, ...), channel_id=2, replica_groups=mesh['dp'=64,'tensor'=2] {'dp'}, use_global_device_ids=true, to_apply=%region_15.16.clone | all-reduce | flops 1186176 | bytes 7110912
  446.3 5.3 fusion.75
  451.7 3.6 fusion.92
  455.3 196.0 %fusion.81 = (f32[16,1536]{1,0:T(8,128)S(1)}, f32[1536,16]{0,1:T(8,128)S(1)}) fusion(f32[768,1536]{1,0:T(8,128)} %fusion.75, f32[1536,768]{0,1:T(8,128)} %fusion.92), kind=kCustom, calls=%all-reduce-scatter.2 | all-reduce-scatter fusion | flops 3145729 | bytes 9634304
  652.7 8.6 collective-permute-start.30
  666.5 6.8 collective-permute-start.25
  676.3 3.1 collective-permute-start.22
  679.5 3.5 collective-permute-start.21
  685.5 3.9 collective-permute-start.19
  689.4 3.6 collective-permute-start.18
  698.4 24.8 %concatenate.28 = bf16[1536,268]{0,1:T(8,128)(2,1)} concatenate(bf16[1536,12]{0,1:T(8,128)(2,1)S(1)} %collective-permute-done.31, bf16[1536,16]{0,1:T(8,128)(2,1)S(1)} %collective-permute-done.30, bf16[1536,16]{0,1:T(8,128)(2,1)S(1)} %collective-permute-done.29, bf16[1536,16]{0,1:T(8,128)(2,1)} %copy-done.23, bf16[1536,16]{0,1:T(8,128)(2,1)} %copy-done.24, ...), dimensions={1} | concatenate | bytes 1695744
  724.9 3.0 collective-permute-start.15
  727.9 4.9 collective-permute-start.14
  736.7 4.8 collective-permute-start.10
  742.9 3.3 collective-permute-start.8
  749.1 4.2 collective-permute-start.5
  753.4 2.8 collective-permute-start.4
  756.2 4.1 collective-permute-start.3
  769.1 24.7 %concatenate.27 = bf16[268,1536]{1,0:T(8,128)(2,1)} concatenate(bf16[12,1536]{1,0:T(8,128)(2,1)S(1)} %collective-permute-done.15, bf16[16,1536]{1,0:T(8,128)(2,1)S(1)} %collective-permute-done.14, bf16[16,1536]{1,0:T(8,128)(2,1)S(1)} %collective-permute-done.13, bf16[16,1536]{1,0:T(8,128)(2,1)S(1)} %collective-permute-done.12, bf16[16,1536]{1,0:T(8,128)(2,1)S(1)} %collective-permute-done.11, ...), dimensions={0} | concatenate | bytes 1695744
  801.8 316.2 %all-reduce.20 = (bf16[768]{0:T(1024)(128)(2,1)S(1)}, bf16[768]{0:T(1024)(128)(2,1)S(1)}, bf16[768]{0:T(1024)(128)(2,1)S(1)}, bf16[768]{0:T(1024)(128)(2,1)S(1)}...) all-reduce(bf16[768]{0:T(1024)(128)(2,1)S(1)} %dynamic-update-slice, ...), channel_id=1, replica_groups=mesh['dp'=64,'tensor'=2] {'dp'}, use_global_device_ids=true, to_apply=%add | all-reduce | flops 5376 | bytes 21504
  1121.7 96.1 %all-gather = bf16[64,3,6]{2,1,0:T(4,128)(2,1)S(1)} all-gather(bf16[1,3,6]{2,1,0:T(4,128)(2,1)S(1)} %fusion.68), channel_id=1, replica_groups=mesh['dp'=64,'tensor'=2] {'dp'}, dimensions={0}, use_global_device_ids=true | all-gather | bytes 2340 | tf_op jit(solution)/shard_map/all_gather | solution.py:224
  1219.6 99.8 %all_gather.39 = bf16[6,64,768]{1,0,2:T(8,128)(2,1)} all-gather(bf16[6,64,12]{1,0,2:T(8,128)(2,1)S(1)} %copy.72), channel_id=1, replica_groups=mesh['dp'=64,'tensor'=2] {'dp'}, dimensions={2}, use_global_device_ids=true | all-gather | bytes 599040 | tf_op jit(solution)/shard_map/all_gather | solution.py:227
  1319.4 2.8 copy.74
  1326.6 5.1 copy.73
  1331.7 5.2 reshape.320
  1336.9 6.0 copy.75
  1343.0 5.2 reshape.306
  (268 shorter events, 89.9 us)
Async XLA Ops:
  8.0 1314.8 %all-reduce.27.cloned.1.call-start = ((), (), s32[]{:S(2)}) async-start(), calls=%async_computation.3 | async-start | bytes 3145728 | tf_op jit(solution)/shard_map/psum | solution.py:132
  58.5 1268.1 %all-gather.7.cloned.1.call-start = ((), (), s32[]{:S(2)}) async-start(), calls=%async_computation | async-start | bytes 3194880 | tf_op jit(solution)/shard_map/all_gather | solution.py:221
  446.3 885.5 %all-gather.11.cloned.1.call-start = ((), (), s32[]{:S(2)}) async-start(), calls=%async_computation.2 | async-start | bytes 3194880 | tf_op jit(solution)/shard_map/all_gather | solution.py:236
  651.4 13.8 %collective-permute-start.31 = (bf16[1536,12]{0,1:T(8,128)(2,1)S(1)}, bf16[1536,12]{0,1:T(8,128)(2,1)S(1)}, u32[]{:S(2)}, u32[]{:S(2)}) collective-permute-start(bf16[1536,12]{0,1:T(8,128)(2,1)S(1)} %slice.115), channel_id=1, source_target_pairs={{0,32},{2,34},{4,36},{6,38},{8,40},{10,42},{12,44},{14,46},{16,48}... | collective-permute-start | bytes 110600
  652.7 13.8 %collective-permute-start.30 = (bf16[1536,16]{0,1:T(8,128)(2,1)S(1)}, bf16[1536,16]{0,1:T(8,128)(2,1)S(1)}, u32[]{:S(2)}, u32[]{:S(2)}) collective-permute-start(bf16[1536,16]{0,1:T(8,128)(2,1)S(1)} %convert.90), channel_id=1, source_target_pairs={{0,30},{2,32},{4,34},{6,36},{8,38},{10,40},{12,42},{14,44},{16,46}... | collective-permute-start | bytes 147464
  661.3 12.1 collective-permute-start.29
  662.6 12.1 collective-permute-start.28
  663.9 12.4 collective-permute-start.27
  665.2 14.3 %collective-permute-start.26 = (bf16[1536,16]{0,1:T(8,128)(2,1)S(1)}, bf16[1536,16]{0,1:T(8,128)(2,1)S(1)}, u32[]{:S(2)}, u32[]{:S(2)}) collective-permute-start(bf16[1536,16]{0,1:T(8,128)(2,1)S(1)} %convert.90), channel_id=1, source_target_pairs={{0,22},{2,24},{4,26},{6,28},{8,30},{10,32},{12,34},{14,36},{16,38}... | collective-permute-start | bytes 147464
  666.5 16.5 %collective-permute-start.25 = (bf16[1536,16]{0,1:T(8,128)(2,1)S(1)}, bf16[1536,16]{0,1:T(8,128)(2,1)S(1)}, u32[]{:S(2)}, u32[]{:S(2)}) collective-permute-start(bf16[1536,16]{0,1:T(8,128)(2,1)S(1)} %convert.90), channel_id=1, source_target_pairs={{0,20},{2,22},{4,24},{6,26},{8,28},{10,30},{12,32},{14,34},{16,36}... | collective-permute-start | bytes 147464
  673.4 12.1 collective-permute-start.24
  674.7 14.7 %collective-permute-start.23 = (bf16[1536,16]{0,1:T(8,128)(2,1)S(1)}, bf16[1536,16]{0,1:T(8,128)(2,1)S(1)}, u32[]{:S(2)}, u32[]{:S(2)}) collective-permute-start(bf16[1536,16]{0,1:T(8,128)(2,1)S(1)} %convert.90), channel_id=1, source_target_pairs={{0,16},{2,18},{4,20},{6,22},{8,24},{10,26},{12,28},{14,30},{16,32}... | collective-permute-start | bytes 147464
  676.3 16.6 %collective-permute-start.22 = (bf16[1536,16]{0,1:T(8,128)(2,1)S(1)}, bf16[1536,16]{0,1:T(8,128)(2,1)S(1)}, u32[]{:S(2)}, u32[]{:S(2)}) collective-permute-start(bf16[1536,16]{0,1:T(8,128)(2,1)S(1)} %convert.90), channel_id=1, source_target_pairs={{0,14},{2,16},{4,18},{6,20},{8,22},{10,24},{12,26},{14,28},{16,30}... | collective-permute-start | bytes 147464
  679.5 15.7 %collective-permute-start.21 = (bf16[1536,16]{0,1:T(8,128)(2,1)S(1)}, bf16[1536,16]{0,1:T(8,128)(2,1)S(1)}, u32[]{:S(2)}, u32[]{:S(2)}) collective-permute-start(bf16[1536,16]{0,1:T(8,128)(2,1)S(1)} %convert.90), channel_id=1, source_target_pairs={{0,12},{2,14},{4,16},{6,18},{8,20},{10,22},{12,24},{14,26},{16,28}... | collective-permute-start | bytes 147464
  683.0 14.8 %collective-permute-start.20 = (bf16[1536,16]{0,1:T(8,128)(2,1)S(1)}, bf16[1536,16]{0,1:T(8,128)(2,1)}, u32[]{:S(2)}, u32[]{:S(2)}) collective-permute-start(bf16[1536,16]{0,1:T(8,128)(2,1)S(1)} %convert.90), channel_id=1, source_target_pairs={{0,10},{2,12},{4,14},{6,16},{8,18},{10,20},{12,22},{14,24},{16,26}... | collective-permute-start | bytes 147464
  685.5 12.4 collective-permute-start.19
  689.4 8.5 collective-permute-start.18
  724.8 618.1 %all-gather.9.cloned.1.call-start = ((), (), s32[]{:S(2)}) async-start(), calls=%async_computation.1 | async-start | bytes 3194880 | tf_op jit(solution)/shard_map/all_gather | solution.py:230
  724.9 11.8 collective-permute-start.15
  727.9 13.7 %collective-permute-start.14 = (bf16[16,1536]{1,0:T(8,128)(2,1)S(1)}, bf16[16,1536]{1,0:T(8,128)(2,1)S(1)}, u32[]{:S(2)}, u32[]{:S(2)}) collective-permute-start(bf16[16,1536]{1,0:T(8,128)(2,1)S(1)} %convert.91), channel_id=1, source_target_pairs={{0,30},{2,32},{4,34},{6,36},{8,38},{10,40},{12,42},{14,44},{16,46}... | collective-permute-start | bytes 147464
  732.8 10.1 collective-permute-start.13
  734.1 12.0 collective-permute-start.12
  735.4 12.4 collective-permute-start.11
  736.7 12.4 collective-permute-start.10
  741.6 11.8 collective-permute-start.9
  742.9 13.3 collective-permute-start.8
  746.2 14.1 %collective-permute-start.7 = (bf16[16,1536]{1,0:T(8,128)(2,1)S(1)}, bf16[16,1536]{1,0:T(8,128)(2,1)S(1)}, u32[]{:S(2)}, u32[]{:S(2)}) collective-permute-start(bf16[16,1536]{1,0:T(8,128)(2,1)S(1)} %convert.91), channel_id=1, source_target_pairs={{0,16},{2,18},{4,20},{6,22},{8,24},{10,26},{12,28},{14,30},{16,32}... | collective-permute-start | bytes 147464
  747.8 15.2 %collective-permute-start.6 = (bf16[16,1536]{1,0:T(8,128)(2,1)S(1)}, bf16[16,1536]{1,0:T(8,128)(2,1)S(1)}, u32[]{:S(2)}, u32[]{:S(2)}) collective-permute-start(bf16[16,1536]{1,0:T(8,128)(2,1)S(1)} %convert.91), channel_id=1, source_target_pairs={{0,14},{2,16},{4,18},{6,20},{8,22},{10,24},{12,26},{14,28},{16,30}... | collective-permute-start | bytes 147464
  749.1 16.5 %collective-permute-start.5 = (bf16[16,1536]{1,0:T(8,128)(2,1)S(1)}, bf16[16,1536]{1,0:T(8,128)(2,1)S(1)}, u32[]{:S(2)}, u32[]{:S(2)}) collective-permute-start(bf16[16,1536]{1,0:T(8,128)(2,1)S(1)} %convert.91), channel_id=1, source_target_pairs={{0,12},{2,14},{4,16},{6,18},{8,20},{10,22},{12,24},{14,26},{16,28}... | collective-permute-start | bytes 147464
  753.4 14.5 %collective-permute-start.4 = (bf16[16,1536]{1,0:T(8,128)(2,1)S(1)}, bf16[16,1536]{1,0:T(8,128)(2,1)S(1)}, u32[]{:S(2)}, u32[]{:S(2)}) collective-permute-start(bf16[16,1536]{1,0:T(8,128)(2,1)S(1)} %convert.91), channel_id=1, source_target_pairs={{0,10},{2,12},{4,14},{6,16},{8,18},{10,20},{12,22},{14,24},{16,26}... | collective-permute-start | bytes 147464
  756.2 11.7 collective-permute-start.3
  760.3 7.6 collective-permute-start.2
  (63 other events, 1265.8 us)
Sparse Core Ops, SparseCore 0:
  58.6 67.3 all-reduce.26
Sparse Core Ops, SparseCore 1:
  446.3 79.1 all-gather.6
  724.9 69.2 all-gather.10
  797.7 67.3 all-gather.8
where the time goes:
time: 1370 us; the launch traced here: 1360 us
  blocking collectives  1080 us (79%)
  local copies, waits for them, and re-layouts  92 us (7%)
  starting transfers between devices  88.3 us (6%)
  matrix products  48.2 us (4%)
  other arithmetic  22.5 us (2%)
  between operations  21 us (2%)
    unnamed x3, blocking collectives  883 us
    all_gather x1, blocking collectives, body(): lax.all_gather(shares[2].astype(jnp.bfloat16), 'dp', axis=2, tiled=True)  99.8 us
    all_gather x1, blocking collectives, body(): lax.all_gather(shares[1].astype(jnp.bfloat16), 'dp', axis=1, tiled=True)  96.1 us
    unnamed x32, starting transfers between devices  88.1 us
    unnamed x150, local copies, waits for them, and re-layouts  78 us
  transfers between devices with their start and end apart: 36, of which 1 were waited for; matrix products, arithmetic and copies ran while one was open for 22% of the time, Pallas kernels for 0%

commit v1 on v0

--- a/solution.py
+++ b/solution.py
@@ -8,6 +8,12 @@
 SEQ = 512
 epsilon = 1e-05
 masked_score = -1000000000.0
+
+
+def unit_treat(x0):
+    return jnp.concatenate(
+        lax.all_to_all(jnp.stack([x0 for _ in range(lax.axis_size("dp"))], 0), "dp", 0, 0), 2
+    )
 
 
 def norm_rows(row_values, gain_vec, shift_vec):
@@ -224,9 +230,7 @@
         lax.all_gather(shares[1].astype(jnp.bfloat16), "dp", axis=1, tiled=True).astype(
             jnp.float32
         ),
-        lax.all_gather(shares[2].astype(jnp.bfloat16), "dp", axis=2, tiled=True).astype(
-            jnp.float32
-        ),
+        unit_treat(shares[2].astype(jnp.bfloat16)).astype(jnp.float32),
         lax.all_gather(shares[3].astype(jnp.bfloat16), "dp", axis=0, tiled=True).astype(
             jnp.float32
         ),

time: 1370 us -> 1240 us (0.905)
  blocking collectives: 1080 us -> 991 us
  local copies, waits for them, and re-layouts: 92 us -> 47.6 us
    all_gather x1 -> x0, blocking collectives: 99.8 us -> none  [body(): lax.all_gather(shares[2].astype(jnp.bfloat16), 'dp', axis=2, tiled=True)]
    unnamed x150 -> x121, local copies, waits for them, and re-layouts: 78 us -> 28.9 us
  transfers between devices with their start and end apart: 36 -> 37, of which waited for: 1 -> 2; matrix products, arithmetic and copies ran while one was open for 22% -> 21% of each run, Pallas kernels for 0% -> 0%
where the time goes in v1:
time: 1240 us; the launch traced here: 1230 us
  blocking collectives  991 us (80%)
  starting transfers between devices  96 us (8%)
  local copies, waits for them, and re-layouts  47.6 us (4%)
  matrix products  46.7 us (4%)
  other arithmetic  22.8 us (2%)
  between operations  21 us (2%)
    unnamed x3, blocking collectives  889 us
    all_gather x1, blocking collectives, body(): lax.all_gather(shares[1].astype(jnp.bfloat16), 'dp', axis=1, tiled=True)  96.1 us
    unnamed x32, starting transfers between devices  88.5 us
    unnamed x121, local copies, waits for them, and re-layouts  28.9 us
  transfers between devices with their start and end apart: 37, of which 2 were waited for; matrix products, arithmetic and copies ran while one was open for 21% of the time, Pallas kernels for 0%

profile of v1, /device:TPU:1, one launch (start us, length us, event | category | flops | bytes accessed | tf_op | source)
XLA Modules:
  0.0 1226.4 jit_solution(12714244955889635307)
XLA Ops:
  13.5 4.4 fusion.88
  29.9 2.6 multiply_convert_fusion
  37.0 9.2 convert_reduce_fusion
  58.4 5.3 fusion.51
  67.5 4.9 all-reduce.21
  72.4 370.6 %all-reduce.28 = (bf16[768]{0:T(1024)(128)(2,1)S(1)}, bf16[768]{0:T(1024)(128)(2,1)S(1)}, bf16[768]{0:T(1024)(128)(2,1)S(1)}, bf16[768]{0:T(1024)(128)(2,1)S(1)}...) all-reduce(bf16[768]{0:T(1024)(128)(2,1)S(1)} %get-tuple-element.14, ...), channel_id=2, replica_groups=mesh['dp'=64,'tensor'=2] {'dp'}, use_global_device_ids=true, to_apply=%region_15.16.clone | all-reduce | flops 1186176 | bytes 7110912
  444.7 5.3 fusion.75
  450.0 3.6 fusion.92
  453.6 195.9 %fusion.81 = (f32[16,1536]{1,0:T(8,128)S(1)}, f32[1536,16]{0,1:T(8,128)S(1)}) fusion(f32[768,1536]{1,0:T(8,128)} %fusion.75, f32[1536,768]{0,1:T(8,128)} %fusion.92), kind=kCustom, calls=%all-reduce-scatter.2 | all-reduce-scatter fusion | flops 3145729 | bytes 9634304
  650.9 9.0 collective-permute-start.30
  665.2 6.8 collective-permute-start.25
  674.9 3.1 collective-permute-start.22
  678.1 3.5 collective-permute-start.21
  683.4 3.9 collective-permute-start.19
  687.3 3.3 collective-permute-start.18
  696.4 2.6 concatenate.28
  699.7 3.5 collective-permute-start.15
  703.3 4.8 collective-permute-start.14
  712.0 5.0 collective-permute-start.10
  718.3 3.1 collective-permute-start.8
  724.4 4.2 collective-permute-start.5
  728.7 2.8 collective-permute-start.4
  731.5 4.0 collective-permute-start.3
  735.5 2.8 collective-permute-start.2
  750.0 7.4 all-to-all-start
  761.1 323.0 %all-reduce.20 = (bf16[768]{0:T(1024)(128)(2,1)S(1)}, bf16[768]{0:T(1024)(128)(2,1)S(1)}, bf16[768]{0:T(1024)(128)(2,1)S(1)}, bf16[768]{0:T(1024)(128)(2,1)S(1)}...) all-reduce(bf16[768]{0:T(1024)(128)(2,1)S(1)} %dynamic-update-slice, ...), channel_id=1, replica_groups=mesh['dp'=64,'tensor'=2] {'dp'}, use_global_device_ids=true, to_apply=%add | all-reduce | flops 5376 | bytes 21504
  1087.1 96.1 %all-gather = bf16[64,3,6]{2,1,0:T(4,128)(2,1)S(1)} all-gather(bf16[1,3,6]{2,1,0:T(4,128)(2,1)S(1)} %fusion.68), channel_id=1, replica_groups=mesh['dp'=64,'tensor'=2] {'dp'}, dimensions={0}, use_global_device_ids=true | all-gather | bytes 2340 | tf_op jit(solution)/shard_map/all_gather | solution.py:230
  1188.1 2.6 reshape.288
  1196.3 5.1 copy.73
  1201.4 5.2 reshape.327
  1206.6 6.2 copy.75
  1212.8 5.2 reshape.313
  (242 shorter events, 90.3 us)
Async XLA Ops:
  8.0 1184.5 %all-reduce.27.cloned.1.call-start = ((), (), s32[]{:S(2)}) async-start(), calls=%async_computation.4 | async-start | bytes 3145728 | tf_op jit(solution)/shard_map/psum | solution.py:138
  58.3 1137.9 %all-gather.7.cloned.1.call-start = ((), (), s32[]{:S(2)}) async-start(), calls=%async_computation.1 | async-start | bytes 3194880 | tf_op jit(solution)/shard_map/all_gather | solution.py:227
  444.6 756.8 %all-gather.11.cloned.1.call-start = ((), (), s32[]{:S(2)}) async-start(), calls=%async_computation.3 | async-start | bytes 3194880 | tf_op jit(solution)/shard_map/all_gather | solution.py:240
  649.6 14.3 %collective-permute-start.31 = (bf16[1536,12]{0,1:T(8,128)(2,1)S(1)}, bf16[1536,12]{0,1:T(8,128)(2,1)S(1)}, u32[]{:S(2)}, u32[]{:S(2)}) collective-permute-start(bf16[1536,12]{0,1:T(8,128)(2,1)S(1)} %slice.115), channel_id=1, source_target_pairs={{0,32},{2,34},{4,36},{6,38},{8,40},{10,42},{12,44},{14,46},{16,48}... | collective-permute-start | bytes 110600
  650.9 14.3 %collective-permute-start.30 = (bf16[1536,16]{0,1:T(8,128)(2,1)S(1)}, bf16[1536,16]{0,1:T(8,128)(2,1)S(1)}, u32[]{:S(2)}, u32[]{:S(2)}) collective-permute-start(bf16[1536,16]{0,1:T(8,128)(2,1)S(1)} %convert.92), channel_id=1, source_target_pairs={{0,30},{2,32},{4,34},{6,36},{8,38},{10,40},{12,42},{14,44},{16,46}... | collective-permute-start | bytes 147464
  659.9 12.1 collective-permute-start.29
  661.2 12.1 collective-permute-start.28
  662.5 12.4 %collective-permute-start.27 = (bf16[1536,16]{0,1:T(8,128)(2,1)S(1)}, bf16[1536,16]{0,1:T(8,128)(2,1)S(1)}, u32[]{:S(2)}, u32[]{:S(2)}) collective-permute-start(bf16[1536,16]{0,1:T(8,128)(2,1)S(1)} %convert.92), channel_id=1, source_target_pairs={{0,24},{2,26},{4,28},{6,30},{8,32},{10,34},{12,36},{14,38},{16,40}... | collective-permute-start | bytes 147464
  663.8 14.2 %collective-permute-start.26 = (bf16[1536,16]{0,1:T(8,128)(2,1)S(1)}, bf16[1536,16]{0,1:T(8,128)(2,1)S(1)}, u32[]{:S(2)}, u32[]{:S(2)}) collective-permute-start(bf16[1536,16]{0,1:T(8,128)(2,1)S(1)} %convert.92), channel_id=1, source_target_pairs={{0,22},{2,24},{4,26},{6,28},{8,30},{10,32},{12,34},{14,36},{16,38}... | collective-permute-start | bytes 147464
  665.2 16.4 %collective-permute-start.25 = (bf16[1536,16]{0,1:T(8,128)(2,1)S(1)}, bf16[1536,16]{0,1:T(8,128)(2,1)S(1)}, u32[]{:S(2)}, u32[]{:S(2)}) collective-permute-start(bf16[1536,16]{0,1:T(8,128)(2,1)S(1)} %convert.92), channel_id=1, source_target_pairs={{0,20},{2,22},{4,24},{6,26},{8,28},{10,30},{12,32},{14,34},{16,36}... | collective-permute-start | bytes 147464
  672.0 11.4 collective-permute-start.24
  673.3 14.0 %collective-permute-start.23 = (bf16[1536,16]{0,1:T(8,128)(2,1)S(1)}, bf16[1536,16]{0,1:T(8,128)(2,1)S(1)}, u32[]{:S(2)}, u32[]{:S(2)}) collective-permute-start(bf16[1536,16]{0,1:T(8,128)(2,1)S(1)} %convert.92), channel_id=1, source_target_pairs={{0,16},{2,18},{4,20},{6,22},{8,24},{10,26},{12,28},{14,30},{16,32}... | collective-permute-start | bytes 147464
  674.9 15.7 %collective-permute-start.22 = (bf16[1536,16]{0,1:T(8,128)(2,1)S(1)}, bf16[1536,16]{0,1:T(8,128)(2,1)S(1)}, u32[]{:S(2)}, u32[]{:S(2)}) collective-permute-start(bf16[1536,16]{0,1:T(8,128)(2,1)S(1)} %convert.92), channel_id=1, source_target_pairs={{0,14},{2,16},{4,18},{6,20},{8,22},{10,24},{12,26},{14,28},{16,30}... | collective-permute-start | bytes 147464
  678.1 15.0 %collective-permute-start.21 = (bf16[1536,16]{0,1:T(8,128)(2,1)S(1)}, bf16[1536,16]{0,1:T(8,128)(2,1)S(1)}, u32[]{:S(2)}, u32[]{:S(2)}) collective-permute-start(bf16[1536,16]{0,1:T(8,128)(2,1)S(1)} %convert.92), channel_id=1, source_target_pairs={{0,12},{2,14},{4,16},{6,18},{8,20},{10,22},{12,24},{14,26},{16,28}... | collective-permute-start | bytes 147464
  681.6 14.3 %collective-permute-start.20 = (bf16[1536,16]{0,1:T(8,128)(2,1)S(1)}, bf16[1536,16]{0,1:T(8,128)(2,1)S(1)}, u32[]{:S(2)}, u32[]{:S(2)}) collective-permute-start(bf16[1536,16]{0,1:T(8,128)(2,1)S(1)} %convert.92), channel_id=1, source_target_pairs={{0,10},{2,12},{4,14},{6,16},{8,18},{10,20},{12,22},{14,24},{16,26}... | collective-permute-start | bytes 147464
  683.4 12.5 %collective-permute-start.19 = (bf16[1536,16]{0,1:T(8,128)(2,1)S(1)}, bf16[1536,16]{0,1:T(8,128)(2,1)S(1)}, u32[]{:S(2)}, u32[]{:S(2)}) collective-permute-start(bf16[1536,16]{0,1:T(8,128)(2,1)S(1)} %convert.92), channel_id=1, source_target_pairs={{0,8},{2,10},{4,12},{6,14},{8,16},{10,18},{12,20},{14,22},{16,24},... | collective-permute-start | bytes 147464
  687.3 8.6 collective-permute-start.18
  699.7 513.1 %all-gather.9.cloned.1.call-start = ((), (), s32[]{:S(2)}) async-start(), calls=%async_computation.2 | async-start | bytes 3194880 | tf_op jit(solution)/shard_map/all_gather | solution.py:234
  699.7 12.3 %collective-permute-start.15 = (bf16[12,1536]{1,0:T(8,128)(2,1)S(1)}, bf16[12,1536]{1,0:T(8,128)(2,1)S(1)}, u32[]{:S(2)}, u32[]{:S(2)}) collective-permute-start(bf16[12,1536]{1,0:T(8,128)(2,1)S(1)} %slice.114), channel_id=1, source_target_pairs={{0,32},{2,34},{4,36},{6,38},{8,40},{10,42},{12,44},{14,46},{16,48}... | collective-permute-start | bytes 110600
  703.3 13.7 %collective-permute-start.14 = (bf16[16,1536]{1,0:T(8,128)(2,1)S(1)}, bf16[16,1536]{1,0:T(8,128)(2,1)S(1)}, u32[]{:S(2)}, u32[]{:S(2)}) collective-permute-start(bf16[16,1536]{1,0:T(8,128)(2,1)S(1)} %convert.93), channel_id=1, source_target_pairs={{0,30},{2,32},{4,34},{6,36},{8,38},{10,40},{12,42},{14,44},{16,46}... | collective-permute-start | bytes 147464
  708.1 10.2 collective-permute-start.13
  709.4 12.0 collective-permute-start.12
  710.7 12.4 %collective-permute-start.11 = (bf16[16,1536]{1,0:T(8,128)(2,1)S(1)}, bf16[16,1536]{1,0:T(8,128)(2,1)S(1)}, u32[]{:S(2)}, u32[]{:S(2)}) collective-permute-start(bf16[16,1536]{1,0:T(8,128)(2,1)S(1)} %convert.93), channel_id=1, source_target_pairs={{0,24},{2,26},{4,28},{6,30},{8,32},{10,34},{12,36},{14,38},{16,40}... | collective-permute-start | bytes 147464
  712.0 12.4 %collective-permute-start.10 = (bf16[16,1536]{1,0:T(8,128)(2,1)S(1)}, bf16[16,1536]{1,0:T(8,128)(2,1)S(1)}, u32[]{:S(2)}, u32[]{:S(2)}) collective-permute-start(bf16[16,1536]{1,0:T(8,128)(2,1)S(1)} %convert.93), channel_id=1, source_target_pairs={{0,22},{2,24},{4,26},{6,28},{8,30},{10,32},{12,34},{14,36},{16,38}... | collective-permute-start | bytes 147464
  717.0 11.6 collective-permute-start.9
  718.3 13.2 %collective-permute-start.8 = (bf16[16,1536]{1,0:T(8,128)(2,1)S(1)}, bf16[16,1536]{1,0:T(8,128)(2,1)S(1)}, u32[]{:S(2)}, u32[]{:S(2)}) collective-permute-start(bf16[16,1536]{1,0:T(8,128)(2,1)S(1)} %convert.93), channel_id=1, source_target_pairs={{0,18},{2,20},{4,22},{6,24},{8,26},{10,28},{12,30},{14,32},{16,34}... | collective-permute-start | bytes 147464
  721.5 14.1 %collective-permute-start.7 = (bf16[16,1536]{1,0:T(8,128)(2,1)S(1)}, bf16[16,1536]{1,0:T(8,128)(2,1)S(1)}, u32[]{:S(2)}, u32[]{:S(2)}) collective-permute-start(bf16[16,1536]{1,0:T(8,128)(2,1)S(1)} %convert.93), channel_id=1, source_target_pairs={{0,16},{2,18},{4,20},{6,22},{8,24},{10,26},{12,28},{14,30},{16,32}... | collective-permute-start | bytes 147464
  723.1 15.2 %collective-permute-start.6 = (bf16[16,1536]{1,0:T(8,128)(2,1)S(1)}, bf16[16,1536]{1,0:T(8,128)(2,1)S(1)}, u32[]{:S(2)}, u32[]{:S(2)}) collective-permute-start(bf16[16,1536]{1,0:T(8,128)(2,1)S(1)} %convert.93), channel_id=1, source_target_pairs={{0,14},{2,16},{4,18},{6,20},{8,22},{10,24},{12,26},{14,28},{16,30}... | collective-permute-start | bytes 147464
  724.4 16.4 %collective-permute-start.5 = (bf16[16,1536]{1,0:T(8,128)(2,1)S(1)}, bf16[16,1536]{1,0:T(8,128)(2,1)S(1)}, u32[]{:S(2)}, u32[]{:S(2)}) collective-permute-start(bf16[16,1536]{1,0:T(8,128)(2,1)S(1)} %convert.93), channel_id=1, source_target_pairs={{0,12},{2,14},{4,16},{6,18},{8,20},{10,22},{12,24},{14,26},{16,28}... | collective-permute-start | bytes 147464
  728.7 14.4 %collective-permute-start.4 = (bf16[16,1536]{1,0:T(8,128)(2,1)S(1)}, bf16[16,1536]{1,0:T(8,128)(2,1)S(1)}, u32[]{:S(2)}, u32[]{:S(2)}) collective-permute-start(bf16[16,1536]{1,0:T(8,128)(2,1)S(1)} %convert.93), channel_id=1, source_target_pairs={{0,10},{2,12},{4,14},{6,16},{8,18},{10,20},{12,22},{14,24},{16,26}... | collective-permute-start | bytes 147464
  731.5 11.6 collective-permute-start.3
  750.0 434.8 %all-to-all-start = ((bf16[64,2,2304]{2,1,0:T(2,128)(2,1)}), bf16[64,2,2304]{2,1,0:T(2,128)(2,1)S(1)}, u32[]{:S(2)}, u32[]{:S(2)}) async-start(bf16[64,2,2304]{2,1,0:T(2,128)(2,1)} %reshape.349), calls=%async_computation | async-start | bytes 1179648 | tf_op jit(solution)/shard_map/all_to_all | solution.py:15
  (48 other events, 940.3 us)
Sparse Core Ops, SparseCore 0:
  58.5 68.0 all-reduce.26
Sparse Core Ops, SparseCore 1:
  444.7 79.4 all-gather.6
  699.8 70.7 all-gather.10
  774.1 68.5 all-gather.8
